TPU v7x, 32 devices: a whole 2x2x4 slice. The times are simulated.
32 devices in a mesh: seq: 8 (over z, y), tile: 4 (over x, core).
Axes of the slice: x: 2, y: 2, z: 4, core: 2. Of those that a mesh axis runs over, the one named last changes fastest.
Arguments:
- queries: bfloat16 [4096, 2048], P(('seq', 'tile')), may hold values from -4.5 to 4.5
- keys: bfloat16 [4096, 2048], P(('seq', 'tile')), may hold values from -4.5 to 4.5
- values: bfloat16 [4096, 2048], P(('seq', 'tile')), may hold values from -6 to 6
- mod_shift: float32 [2048], replicated, may hold values from -4 to 4
- mod_scale: float32 [2048], replicated, may hold values from -2 to 2
- final_weight: float32 [2048, 64], replicated, may hold values from -0.125 to 0.125
- final_bias: float32 [64], replicated, may hold values from -3 to 3
- tile_widths: int32 [4], replicated, may hold values from 1 to 24, 64 in all
- conv_in_weight: bfloat16 [432, 512], replicated, may hold values from -0.3125 to 0.3125
- conv_in_bias: float32 [512], replicated, may hold values from -3 to 3
- conv_up_weight: bfloat16 [9, 512, 256], replicated, may hold values from -0.09375 to 0.09375
- conv_up_bias: float32 [256], replicated, may hold values from -3 to 3
Outputs:
- pixels: bfloat16 [8, 64, 128, 256], P('seq', None, 'tile')
Inputs may be any that keep to these rules, and one draw needn't show every extreme that they name: `tile_widths`: tile widths sum to 64; the widest is exactly 24.
All inputs are finite; a program needn't handle non-finite values.
Results may differ from a plain program's by a relative error of at most 0.011.
Values may be sent and summed in bfloat16 or wider, within the bound.
A program may use at most 128 MiB of HBM per device.

v0:
```python
import functools

import jax
import jax.numpy as jnp
from jax import lax
from jax.experimental import pallas as pl
from jax.experimental.pallas import tpu as pltpu
from jax.sharding import PartitionSpec as P

HD = 128
PR = 16
PC = 32
OV = 2
CB = 8
QB = 256
GROUPS = 4
VMEM_LIMIT = 56 * 1024 * 1024
MESH = pl.DeviceIdType.MESH


def attention_kernel(
    dims,
    q_ref,
    k_ref,
    v_ref,
    shift_ref,
    scale_ref,
    fw_ref,
    fb_ref,
    lat_ref,
    q_buf,
    k_buf,
    v_buf,
    top,
    acc,
    o_buf,
    att,
    out_patch,
    in_patch,
    local_sem,
    send_sem,
    recv_sem,
    relay_send,
    relay_recv,
    patch_send,
    patch_recv,
):
    heads, nseq, ntile, needed, own = dims
    ndev = nseq * ntile
    members = ndev // heads
    count = q_ref.shape[0]
    s = lax.axis_index("seq")
    t = lax.axis_index("tile")
    me = s * ntile + t
    rank = lax.div(me, members)
    side = lax.rem(me, members)

    def place(device):
        return (lax.div(device, ntile), lax.rem(device, ntile))

    def peer(r):
        return place(lax.rem(r + heads, heads) * members + side)

    def columns(h):
        return pl.ds(pl.multiple_of(h * HD, HD), HD)

    barrier = pltpu.get_barrier_semaphore()

    @pl.loop(1, ndev)
    def _(i):
        pl.semaphore_signal(
            barrier, inc=1, device_id=place(lax.rem(me + i, ndev)), device_id_type=MESH
        )

    pl.semaphore_wait(barrier, ndev - 1)

    targets = (
        lambda off: q_buf.at[off],
        lambda off: k_buf.at[side, off],
        lambda off: v_buf.at[side, off, :, 0:HD],
    )
    sources = (q_ref, k_ref, v_ref)

    def outgoing(kind, off):
        h = lax.rem(rank + off, heads)
        return pltpu.make_async_remote_copy(
            src_ref=sources[kind].at[:, columns(h)],
            dst_ref=targets[kind](off),
            send_sem=send_sem.at[kind, off],
            recv_sem=recv_sem.at[kind, off],
            device_id=peer(rank + off),
            device_id_type=MESH,
        )

    locals_ = [
        pltpu.make_async_copy(
            sources[kind].at[:, columns(rank)], targets[kind](0), local_sem.at[kind]
        )
        for kind in range(3)
    ]
    for copy in locals_:
        copy.start()

    @pl.loop(1, heads)
    def _(off):
        outgoing(0, off).start()

    @pl.loop(1, heads)
    def _(off):
        outgoing(1, off).start()
        outgoing(2, off).start()

    v_buf[:, :, :, HD:] = jnp.ones_like(v_buf[:, :, :, HD:])
    top[...] = jnp.full_like(top, -1e30)
    acc[...] = jnp.zeros_like(acc)
    for copy in locals_:
        copy.wait()

    @pl.loop(1, heads)
    def _(off):
        outgoing(0, off).wait_recv()

    def relay(kind, part, other):
        slots = pl.ds(part * per, per)
        ref = (None, k_buf.at[side, slots], v_buf.at[side, slots, :, 0:HD])[kind]
        return pltpu.make_async_remote_copy(
            src_ref=ref,
            dst_ref=ref,
            send_sem=relay_send.at[kind - 1, part, other],
            recv_sem=relay_recv.at[kind - 1, part, other],
            device_id=place(rank * members + lax.rem(side + other, members)),
            device_id_type=MESH,
        )

    def relayed(kind, part, other):
        slots = pl.ds(part * per, per)
        origin = lax.rem(side - other + members, members)
        ref = (None, k_buf.at[origin, slots], v_buf.at[origin, slots, :, 0:HD])[kind]
        return pltpu.make_async_remote_copy(
            src_ref=ref,
            dst_ref=ref,
            send_sem=relay_send.at[kind - 1, part, other],
            recv_sem=relay_recv.at[kind - 1, part, other],
            device_id=place(rank * members + lax.rem(side + other, members)),
            device_id_type=MESH,
        )

    def give_back(off):
        return pltpu.make_async_remote_copy(
            src_ref=o_buf.at[off],
            dst_ref=att.at[rank],
            send_sem=send_sem.at[3, off],
            recv_sem=recv_sem.at[3, off],
            device_id=peer(rank - off),
            device_id_type=MESH,
        )

    def returned(off):
        return pltpu.make_async_remote_copy(
            src_ref=o_buf.at[off],
            dst_ref=att.at[lax.rem(rank + off, heads)],
            send_sem=send_sem.at[3, off],
            recv_sem=recv_sem.at[3, off],
            device_id=peer(rank - off),
            device_id_type=MESH,
        )

    per = heads // GROUPS
    factor = HD**-0.5 * 1.4426950408889634
    width = QB // count
    for part in range(GROUPS):
        first = max(part * per, 1)

        @pl.loop(first, (part + 1) * per)
        def _(off):
            outgoing(1, off).wait_recv()
            outgoing(2, off).wait_recv()

        for other in range(1, members):
            relay(1, part, other).start()
            relay(2, part, other).start()
        for other in range(1, members):
            relayed(1, part, other).wait_recv()
            relayed(2, part, other).wait_recv()

        @pl.loop(0, heads // width)
        def _(i):
            rows = pl.ds(pl.multiple_of(i * QB, QB), QB)
            q = q_buf[pl.ds(i * width, width)].reshape(QB, HD)
            keys = k_buf[:, part * per : (part + 1) * per].reshape(-1, HD)
            vals = v_buf[:, part * per : (part + 1) * per].reshape(-1, 2 * HD)
            scores = lax.dot_general(
                q, keys, (((1,), (1,)), ((), ())), preferred_element_type=jnp.float32
            )
            old = top[rows, :]
            new = jnp.maximum(old, jnp.max(scores, axis=1, keepdims=True))
            probs = jnp.exp2((scores - new[:, 0:1]) * factor).astype(jnp.bfloat16)
            fade = jnp.exp2((old - new) * factor)
            total = acc[rows, :] * jnp.concatenate([fade, fade], axis=1) + jnp.dot(
                probs, vals, preferred_element_type=jnp.float32
            )
            if part < GROUPS - 1:
                top[rows, :] = new
                acc[rows, :] = total
            else:
                o = (total[:, 0:HD] / total[:, HD:]).astype(jnp.bfloat16)
                o_buf[pl.ds(i * width, width)] = o.reshape(width, count, HD)
                for j in range(width):
                    off = i * width + j

                    @pl.when(off > 0)
                    def _():
                        give_back(off).start()

    att[rank] = o_buf[0]

    @pl.loop(1, heads)
    def _(off):
        returned(off).wait_recv()

    feats = [att[h].astype(jnp.float32) for h in range(heads)]
    mean = jnp.sum(sum(feats), axis=1, keepdims=True) / (heads * HD)
    devs = [x - mean for x in feats]
    var = jnp.sum(sum(d * d for d in devs), axis=1, keepdims=True) / (heads * HD)
    inv = 1.0 / jnp.sqrt(var + 1e-06)
    normed = jnp.concatenate(
        [
            devs[h] * inv * (1.0 + scale_ref[h : h + 1, :]) + shift_ref[h : h + 1, :]
            for h in range(heads)
        ],
        axis=1,
    )
    patches = (
        jnp.dot(
            normed,
            fw_ref[...],
            precision=lax.Precision.HIGHEST,
            preferred_element_type=jnp.float32,
        )
        + fb_ref[...]
    )
    patches = jnp.concatenate([patches, patches], axis=1)
    col = lax.rem(lax.broadcasted_iota(jnp.int32, patches.shape, 0), PC)
    shifted = (
        jnp.where(col == 0, 0.0, pltpu.roll(patches, 1, 0)),
        patches,
        jnp.where(col == PC - 1, 0.0, pltpu.roll(patches, count - 1, 0)),
    )
    lines = count // PC
    for sh in range(3):
        grid = shifted[sh].reshape(lines, PC, 2 * 64)
        if own < CB:
            grid = jnp.concatenate([grid, jnp.zeros((lines, CB, 2 * 64), jnp.float32)], axis=1)
        for tp in range(ntile):
            out_patch[tp, sh] = (
                grid[:, own * tp : own * tp + CB].reshape(lines * CB, 2 * 64).astype(jnp.bfloat16)
            )

    def patch_copy(dist, step, incoming=False):
        tp = lax.rem(t + step, ntile)
        origin = lax.rem(t - step + ntile, ntile) if incoming else t
        return pltpu.make_async_remote_copy(
            src_ref=out_patch.at[tp],
            dst_ref=in_patch.at[needed - dist, origin],
            send_sem=patch_send.at[dist, step],
            recv_sem=patch_recv.at[dist, step],
            device_id=(lax.rem(s + dist, nseq), tp),
            device_id_type=MESH,
        )

    for dist in reversed(range(needed + 1)):

        @pl.when(s + dist < nseq)
        def _():
            @pl.loop(0 if dist else 1, ntile)
            def _(step):
                patch_copy(dist, step).start()

    in_patch[needed, t] = out_patch[t]
    for dist in range(needed + 1):

        @pl.when(s >= dist)
        def _():
            @pl.loop(0 if dist else 1, ntile)
            def _(step):
                patch_copy(dist, step, True).wait_recv()

            lat_ref[needed - dist] = in_patch[needed - dist]

        @pl.when(s < dist)
        def _():
            lat_ref[needed - dist] = jnp.zeros_like(lat_ref[needed - dist])

    @pl.loop(1, heads)
    def _(off):
        for kind in range(3):
            outgoing(kind, off).wait_send()
        give_back(off).wait_send()

    for part in range(GROUPS):
        for other in range(1, members):
            relay(1, part, other).wait_send()
            relay(2, part, other).wait_send()
    for dist in range(needed + 1):

        @pl.when(s + dist < nseq)
        def _():
            @pl.loop(0 if dist else 1, ntile)
            def _(step):
                patch_copy(dist, step).wait_send()


def prepare_weights(win_ref, wup_ref, wx, wph):
    wx[...] = jnp.zeros_like(wx)
    for a in range(2):
        for b in range(2):
            for kx in range(3):
                half = (b + kx - 1) % 2
                for kt in range(3):
                    for i in range(2):
                        for line in range(2):
                            ky = 2 * (i - 1 + a) + line - a + 1
                            if 0 <= ky <= 2:
                                to = kt * 128 + i * 64 + (line * 2 + half) * 16
                                at = ((kt * 3 + ky) * 3 + kx) * 16
                                wx[a, b, kx, to : to + 16, :] = win_ref[at : at + 16, :]
    taps = (((0,), (1, 2)), ((0, 1), (2,)))
    for a in range(2):
        for b in range(2):
            for ty in range(2):
                for tx in range(2):
                    parts = [
                        wup_ref[ky * 3 + kx].astype(jnp.float32)
                        for ky in taps[a][ty]
                        for kx in taps[b][tx]
                    ]
                    wph[a, b, ty * 2 + tx] = sum(parts[1:], parts[0]).astype(jnp.bfloat16)


def conv_kernel(
    dims,
    tile_ref,
    widths_ref,
    lat_ref,
    win_ref,
    bin_ref,
    wup_ref,
    bup_ref,
    out_ref,
    wx,
    wph,
    mixed,
    wide,
    hidden,
    coef,
    cut,
):
    ntile, frames, lines, own = dims
    t = tile_ref[0]
    prepare_weights(win_ref, wup_ref, wx, wph)

    col = lax.broadcasted_iota(jnp.int32, (CB, 128), 0) + own * t
    starts, spans = [], []
    begin = jnp.int32(0)
    for k in range(ntile):
        starts.append(begin - OV)
        spans.append(widths_ref[k] + 2 * OV)
        begin = begin + widths_ref[k]
    for b in range(2):
        for px in range(2):
            x = 4 * col + 2 * b + px
            ramps = []
            for k in range(ntile):
                u = x - 2 * starts[k]
                dist = jnp.minimum(u, 2 * spans[k] - 1 - u) + 1
                ramps.append(jnp.clip(dist, 0, 4 * OV).astype(jnp.float32))
            scale = 1.0 / sum(ramps)
            for tx in range(2):
                full = left = right = jnp.zeros((CB, 128), jnp.float32)
                for k in range(ntile):
                    j = 2 * col + b + tx - 1 + px - starts[k]
                    share = ramps[k] * scale
                    left = left + jnp.where(j == 0, share, 0.0)
                    right = right + jnp.where(j == spans[k] - 1, share, 0.0)
                    full = full + jnp.where((j > 0) & (j < spans[k] - 1), share, 0.0)
                for v, c in enumerate((full, left, right)):
                    coef[b, px, tx, v] = c

    rows = PR * CB
    cut[...] = jnp.zeros_like(cut)
    lane = lax.broadcasted_iota(jnp.int32, (rows, 128), 1)
    blocks = PR // lines
    pad = jnp.zeros((CB, 128), jnp.float32)

    for frame in range(frames):
        first = lat_ref.shape[0] * frames - frames - 2 + frame
        for sh in range(3):
            pieces = ([], [])
            for kt in range(3):
                slot, inner = divmod(first + kt, frames)
                x = jnp.concatenate(
                    [lat_ref[slot, inner * blocks + i, sh] for i in range(blocks)], axis=0
                ).astype(jnp.float32)
                above = jnp.concatenate([pad, x[:-CB]], axis=0)
                below = jnp.concatenate([x[CB:], pad], axis=0)
                pieces[0].append(jnp.where(lane < 64, above, x).astype(jnp.bfloat16))
                pieces[1].append(jnp.where(lane < 64, x, below).astype(jnp.bfloat16))
            for a in range(2):
                cut[a, sh] = jnp.concatenate(pieces[a], axis=1)

        for a in range(2):
            for b in range(2):
                for kx in range(3):
                    low = (b + kx - 1) // 2 + 1 - b
                    source = jnp.concatenate([cut[a, low], cut[a, low + 1]], axis=0)
                    hidden[kx] = jnp.dot(
                        source, wx[a, b, kx], preferred_element_type=jnp.float32
                    ).reshape(2, PR, CB, -1)

                @pl.loop(0, PR)
                def _(r):
                    left, middle, right = (hidden[kx, :, r] for kx in range(3))
                    middle = middle + bin_ref[...][None]
                    hidden[0, :, r] = jax.nn.silu(left + middle + right)
                    hidden[1, :, r] = jax.nn.silu(middle + right)
                    hidden[2, :, r] = jax.nn.silu(left + middle)

                for hi in range(2):
                    place = 2 * hi - b
                    for ob in range(2):
                        for px in range(2):
                            tx = place + 1 - ob - px
                            if tx not in (0, 1):
                                continue
                            for part in range(0, hidden.shape[-1], 128):
                                lanes = slice(part, part + 128)
                                value = hidden[0, hi, :, :, lanes] * coef[ob, px, tx, 0][None]
                                for v in (1, 2):
                                    value = (
                                        value
                                        + hidden[v, hi, :, :, lanes] * coef[ob, px, tx, v][None]
                                    )
                                gone = jnp.zeros((1,) + value.shape[1:], jnp.float32)
                                if a == 0:
                                    moved = jnp.concatenate([value[1:], gone], axis=0)
                                    spots = (1, 3)
                                else:
                                    moved = jnp.concatenate([gone, value[:-1]], axis=0)
                                    spots = (2, 0)
                                for spot, val in zip(spots, (value, moved)):
                                    mixed[ob, px, tx, spot, :, lanes] = val.reshape(
                                        rows, 128
                                    ).astype(jnp.bfloat16)

        for ya in range(2):
            for px in range(2):
                total = None
                for ty in range(2):
                    for tx in range(2):
                        source = jnp.concatenate(
                            [
                                mixed[b, px, tx, a + ty + ya]
                                for a in range(2)
                                for b in range(2)
                            ],
                            axis=0,
                        )
                        term = jnp.dot(
                            source, wph[ya, px, ty * 2 + tx], preferred_element_type=jnp.float32
                        )
                        total = term if total is None else total + term
                total = (total + bup_ref[...]).reshape(2, 2, PR, CB, -1)
                for a in range(2):
                    for b in range(2):
                        for half in range(2):
                            wide[
                                half, :, 2 * a + ya, pl.ds(2 * b + px, CB, stride=4), :
                            ] = total[a, b, :, :, half * 128 : (half + 1) * 128]
        for half in range(2):
            out_ref[frame, :, :, half * 128 : (half + 1) * 128] = (
                wide[half, :, :, 0 : 4 * own, :]
                .reshape(4 * PR, 4 * own, -1)
                .astype(jnp.bfloat16)
            )


def per_device(
    queries,
    keys,
    values,
    mod_shift,
    mod_scale,
    final_weight,
    final_bias,
    tile_widths,
    conv_in_weight,
    conv_in_bias,
    conv_up_weight,
    conv_up_bias,
):
    nseq, ntile = lax.axis_size("seq"), lax.axis_size("tile")
    count, feat = queries.shape
    heads = feat // HD
    ndev = nseq * ntile
    members = ndev // heads
    lines = count // PC
    frames = count * ntile // (PR * PC)
    needed = -(-2 // frames)
    own = PC // ntile
    vmem = pl.BlockSpec(memory_space=pltpu.VMEM)
    lat_shape = (needed + 1, ntile, 3, lines * CB, 128)
    lat = pl.pallas_call(
        functools.partial(attention_kernel, (heads, nseq, ntile, needed, own)),
        out_shape=jax.ShapeDtypeStruct(lat_shape, jnp.bfloat16),
        in_specs=[vmem] * 7,
        out_specs=vmem,
        scratch_shapes=[
            pltpu.VMEM((heads, count, HD), jnp.bfloat16),
            pltpu.VMEM((members, heads, count, HD), jnp.bfloat16),
            pltpu.VMEM((members, heads, count, 2 * HD), jnp.bfloat16),
            pltpu.VMEM((heads * count, HD), jnp.float32),
            pltpu.VMEM((heads * count, 2 * HD), jnp.float32),
            pltpu.VMEM((heads, count, HD), jnp.bfloat16),
            pltpu.VMEM((heads, count, HD), jnp.bfloat16),
            pltpu.VMEM(lat_shape[1:], jnp.bfloat16),
            pltpu.VMEM(lat_shape, jnp.bfloat16),
            pltpu.SemaphoreType.DMA((3,)),
            pltpu.SemaphoreType.DMA((4, heads)),
            pltpu.SemaphoreType.DMA((4, heads)),
            pltpu.SemaphoreType.DMA((2, GROUPS, members)),
            pltpu.SemaphoreType.DMA((2, GROUPS, members)),
            pltpu.SemaphoreType.DMA((needed + 1, ntile)),
            pltpu.SemaphoreType.DMA((needed + 1, ntile)),
        ],
        compiler_params=pltpu.CompilerParams(
            collective_id=0, has_side_effects=True, vmem_limit_bytes=VMEM_LIMIT
        ),
    )(
        queries,
        keys,
        values,
        mod_shift.reshape(heads, HD),
        mod_scale.reshape(heads, HD),
        final_weight,
        final_bias.reshape(1, -1),
    )
    ch_in, ch_out = conv_up_weight.shape[1:]
    return pl.pallas_call(
        functools.partial(conv_kernel, (ntile, frames, lines, own)),
        out_shape=jax.ShapeDtypeStruct((frames, 4 * PR, 4 * own, ch_out), jnp.bfloat16),
        in_specs=[pl.BlockSpec(memory_space=pltpu.SMEM)] * 2 + [vmem] * 5,
        out_specs=vmem,
        scratch_shapes=[
            pltpu.VMEM((2, 2, 3, 384, ch_in), jnp.bfloat16),
            pltpu.VMEM((2, 2, 4, ch_in, ch_out), jnp.bfloat16),
            pltpu.VMEM((2, 2, 2, 4, PR * CB, ch_in), jnp.bfloat16),
            pltpu.VMEM((2, PR, 4, 4 * CB, 128), jnp.float32),
            pltpu.VMEM((3, 2, PR, CB, ch_in), jnp.float32),
            pltpu.VMEM((2, 2, 2, 3, CB, 128), jnp.float32),
            pltpu.VMEM((2, 3, PR * CB, 384), jnp.bfloat16),
        ],
        compiler_params=pltpu.CompilerParams(vmem_limit_bytes=VMEM_LIMIT),
    )(
        lax.axis_index("tile").reshape(1),
        tile_widths,
        lat,
        conv_in_weight,
        conv_in_bias.reshape(1, -1),
        conv_up_weight,
        conv_up_bias.reshape(1, -1),
    )


def solution(mesh):
    return jax.shard_map(
        per_device,
        mesh=mesh,
        in_specs=(P(("seq", "tile"), None),) * 3 + (P(),) * 9,
        out_specs=P("seq", None, "tile", None),
        check_vma=False,
    )
```

profile of v0, /device:TPU:9, one launch (start us, length us, event | category | flops | bytes accessed | tf_op | source)
XLA Modules:
  0.0 101.5 jit_solution(5160894775822968065)
XLA Ops:
  0.0 2.4 %copy.13.fw_ref = f32[2048,64]{1,0:T(8,128)} copy(f32[2048,64]{0,1:T(8,128)} %param.17) | data formatting | bytes 1048576 | tf_op args[5]
  2.4 87.5 %shard_map.118.lat_ref = bf16[3,4,3,32,128]{4,3,2,1,0:T(8,128)(2,1)} custom-call(bf16[128,2048]{1,0:T(8,128)(2,1)} %q_ref.1, bf16[128,2048]{1,0:T(8,128)(2,1)} %k_ref.1, bf16[128,2048]{1,0:T(8,128)(2,1)} %v_ref.1, f32[16,128]{1,0:T(8,128)} %bitcast.6, f32[16,128]{1,0:T(8,128)} %bitcast.7, f32[2048,64]{1,0:T(8,128)} %copy.13.fw_ref, f32[1,64]{1,0:T(1,128)} %bitcast.10), custom_call_target="tpu_custom_call" | custom-call | tf_op jit(solution)/shard_map/pallas_call | solution.py:512
  89.8 11.7 %shard_map.119 = bf16[1,64,32,256]{3,2,1,0:T(8,128)(2,1)} custom-call(s32[1]{0:T(128)} %bitcast.tile_ref, s32[4]{0:T(128)} %widths_ref.1, bf16[3,4,3,32,128]{4,3,2,1,0:T(8,128)(2,1)} %shard_map.118.lat_ref, bf16[432,512]{1,0:T(8,128)(2,1)} %win_ref.1, f32[1,512]{1,0:T(1,128)} %bitcast.8, bf16[9,512,256]{2,1,0:T(8,128)(2,1)} %wup_ref.1, f32[1,256]{1,0:T(1,128)} %bitcast.9), custom_call_target="tpu_custom_call" | custom-call | tf_op jit(solution)/shard_map/pallas_call | solution.py:548
where the time goes:
time: 103 us; the launch traced here: 102 us
  Pallas kernels  99.2 us (96%)
  local copies, waits for them, and re-layouts  2.35 us (2%)
    pallas_call x1, Pallas kernels, per_device(): pl.pallas_call(functools.partial(attention_kernel, (heads, nseq, ntile, n...  87.5 us
    pallas_call x1, Pallas kernels, per_device(): pl.pallas_call(functools.partial(conv_kernel, (ntile, frames, lines, own)...  11.7 us
    unnamed x1, local copies, waits for them, and re-layouts  2.35 us

commit v1 on v0

--- a/solution.py
+++ b/solution.py
@@ -61,6 +61,12 @@
     def peer(r):
         return place(lax.rem(r + heads, heads) * members + side)
 
+    def mixed(x, y):
+        bits = heads.bit_length() - 1
+        return sum(
+            lax.rem(lax.div(x, 1 << i) + lax.div(y, 1 << i), 2) * (1 << i) for i in range(bits)
+        )
+
     def columns(h):
         return pl.ds(pl.multiple_of(h * HD, HD), HD)
 
@@ -82,13 +88,13 @@
     sources = (q_ref, k_ref, v_ref)
 
     def outgoing(kind, off):
-        h = lax.rem(rank + off, heads)
+        h = mixed(rank, off)
         return pltpu.make_async_remote_copy(
             src_ref=sources[kind].at[:, columns(h)],
             dst_ref=targets[kind](off),
             send_sem=send_sem.at[kind, off],
             recv_sem=recv_sem.at[kind, off],
-            device_id=peer(rank + off),
+            device_id=peer(mixed(rank, off)),
             device_id_type=MESH,
         )
 
@@ -102,7 +108,8 @@
         copy.start()
 
     @pl.loop(1, heads)
-    def _(off):
+    def _(o):
+        off = heads - o
         outgoing(0, off).start()
 
     @pl.loop(1, heads)
@@ -151,17 +158,17 @@
             dst_ref=att.at[rank],
             send_sem=send_sem.at[3, off],
             recv_sem=recv_sem.at[3, off],
-            device_id=peer(rank - off),
+            device_id=peer(mixed(rank, off)),
             device_id_type=MESH,
         )
 
     def returned(off):
         return pltpu.make_async_remote_copy(
             src_ref=o_buf.at[off],
-            dst_ref=att.at[lax.rem(rank + off, heads)],
+            dst_ref=att.at[mixed(rank, off)],
             send_sem=send_sem.at[3, off],
             recv_sem=recv_sem.at[3, off],
-            device_id=peer(rank - off),
+            device_id=peer(mixed(rank, off)),
             device_id_type=MESH,
         )
 
@@ -183,7 +190,7 @@
             relayed(1, part, other).wait_recv()
             relayed(2, part, other).wait_recv()
 
-        @pl.loop(0, heads // width)
+        @pl.loop(0, heads // width, unroll=2)
         def _(i):
             rows = pl.ds(pl.multiple_of(i * QB, QB), QB)
             q = q_buf[pl.ds(i * width, width)].reshape(QB, HD)
@@ -231,9 +238,10 @@
         axis=1,
     )
     patches = (
-        jnp.dot(
+        lax.dot_general(
             normed,
             fw_ref[...],
+            (((1,), (1,)), ((), ())),
             precision=lax.Precision.HIGHEST,
             preferred_element_type=jnp.float32,
         )
@@ -541,7 +549,7 @@
         values,
         mod_shift.reshape(heads, HD),
         mod_scale.reshape(heads, HD),
-        final_weight,
+        final_weight.T,
         final_bias.reshape(1, -1),
     )
     ch_in, ch_out = conv_up_weight.shape[1:]

time: 103 us -> 84.5 us (0.82)
  the two profiles are of different devices: /device:TPU:9 before, /device:TPU:17 now
where the time goes in v1:
time: 84.5 us; the launch traced here: 84.4 us
  Pallas kernels  84.4 us (100%)
    pallas_call x1, Pallas kernels, per_device(): pl.pallas_call(functools.partial(attention_kernel, (heads, nseq, ntile, n...  72.7 us
    pallas_call x1, Pallas kernels, per_device(): pl.pallas_call(functools.partial(conv_kernel, (ntile, frames, lines, own)...  11.7 us

profile of v1, /device:TPU:17, one launch (start us, length us, event | category | flops | bytes accessed | tf_op | source)
XLA Modules:
  0.0 84.4 jit_solution(5507338183507397834)
XLA Ops:
  0.0 72.7 %shard_map.118.lat_ref = bf16[3,4,3,32,128]{4,3,2,1,0:T(8,128)(2,1)} custom-call(bf16[128,2048]{1,0:T(8,128)(2,1)} %q_ref.1, bf16[128,2048]{1,0:T(8,128)(2,1)} %k_ref.1, bf16[128,2048]{1,0:T(8,128)(2,1)} %v_ref.1, f32[16,128]{1,0:T(8,128)} %bitcast.8, f32[16,128]{1,0:T(8,128)} %bitcast.9, f32[64,2048]{1,0:T(8,128)} %bitcast.7, f32[1,64]{1,0:T(1,128)} %bitcast.12), custom_call_target="tpu_custom_call" | custom-call | tf_op jit(solution)/shard_map/pallas_call | solution.py:520
  72.7 11.7 %shard_map.119 = bf16[1,64,32,256]{3,2,1,0:T(8,128)(2,1)} custom-call(s32[1]{0:T(128)} %bitcast.tile_ref, s32[4]{0:T(128)} %widths_ref.1, bf16[3,4,3,32,128]{4,3,2,1,0:T(8,128)(2,1)} %shard_map.118.lat_ref, bf16[432,512]{1,0:T(8,128)(2,1)} %win_ref.1, f32[1,512]{1,0:T(1,128)} %bitcast.10, bf16[9,512,256]{2,1,0:T(8,128)(2,1)} %wup_ref.1, f32[1,256]{1,0:T(1,128)} %bitcast.11), custom_call_target="tpu_custom_call" | custom-call | tf_op jit(solution)/shard_map/pallas_call | solution.py:556

commit v2 on v1

--- a/solution.py
+++ b/solution.py
@@ -191,7 +191,8 @@
             relayed(2, part, other).wait_recv()
 
         @pl.loop(0, heads // width, unroll=2)
-        def _(i):
+        def _(turn):
+            i = heads // width - 1 - turn
             rows = pl.ds(pl.multiple_of(i * QB, QB), QB)
             q = q_buf[pl.ds(i * width, width)].reshape(QB, HD)
             keys = k_buf[:, part * per : (part + 1) * per].reshape(-1, HD)

time: 84.5 us -> 81.6 us (0.966)
  the two profiles are of different devices: /device:TPU:17 before, /device:TPU:9 now
where the time goes in v2:
time: 81.6 us; the launch traced here: 81.4 us
  Pallas kernels  81.4 us (100%)
    pallas_call x1, Pallas kernels, per_device(): pl.pallas_call(functools.partial(attention_kernel, (heads, nseq, ntile, n...  69.7 us
    pallas_call x1, Pallas kernels, per_device(): pl.pallas_call(functools.partial(conv_kernel, (ntile, frames, lines, own)...  11.7 us

profile of v2, /device:TPU:9, one launch (start us, length us, event | category | flops | bytes accessed | tf_op | source)
XLA Modules:
  0.0 81.4 jit_solution(12331277518689374169)
XLA Ops:
  0.0 69.7 %shard_map.118.lat_ref = bf16[3,4,3,32,128]{4,3,2,1,0:T(8,128)(2,1)} custom-call(bf16[128,2048]{1,0:T(8,128)(2,1)} %q_ref.1, bf16[128,2048]{1,0:T(8,128)(2,1)} %k_ref.1, bf16[128,2048]{1,0:T(8,128)(2,1)} %v_ref.1, f32[16,128]{1,0:T(8,128)} %bitcast.8, f32[16,128]{1,0:T(8,128)} %bitcast.9, f32[64,2048]{1,0:T(8,128)} %bitcast.7, f32[1,64]{1,0:T(1,128)} %bitcast.12), custom_call_target="tpu_custom_call" | custom-call | tf_op jit(solution)/shard_map/pallas_call | solution.py:521
  69.7 11.7 %shard_map.119 = bf16[1,64,32,256]{3,2,1,0:T(8,128)(2,1)} custom-call(s32[1]{0:T(128)} %bitcast.tile_ref, s32[4]{0:T(128)} %widths_ref.1, bf16[3,4,3,32,128]{4,3,2,1,0:T(8,128)(2,1)} %shard_map.118.lat_ref, bf16[432,512]{1,0:T(8,128)(2,1)} %win_ref.1, f32[1,512]{1,0:T(1,128)} %bitcast.10, bf16[9,512,256]{2,1,0:T(8,128)(2,1)} %wup_ref.1, f32[1,256]{1,0:T(1,128)} %bitcast.11), custom_call_target="tpu_custom_call" | custom-call | tf_op jit(solution)/shard_map/pallas_call | solution.py:557
